TPU v7x, 32 devices: a whole 2x2x4 slice. The times are simulated.
32 devices in a mesh: group: 2 (over y), dp: 16 (over z, x, core).
Axes of the slice: x: 2, y: 2, z: 4, core: 2. Of those that a mesh axis runs over, the one named last changes fastest.
Arguments:
- clips_feat: bfloat16 [4096, 4096], P(('group', 'dp')), parts along dimension 0, may hold values from -6 to 6
- weight: bfloat16 [4096, 384], P('dp'), may hold values from -0.09375 to 0.09375
- sentences: bfloat16 [4096, 384], P(('group', 'dp')), parts along dimension 0, may hold values from -6 to 6
- log_scale: float32 [1], replicated, may hold values from 4.3 to 4.6
- bias: float32 [1], replicated, may hold values from -14 to -11
- positives: int32 [4096, 2], P(('group', 'dp')), parts along dimension 0, may hold values from 0 to 2047
Outputs:
- clip_loss: float32 [4096], P(('group', 'dp')), parts along dimension 0
- grad_weight: float32 [8192, 384], P(('group', 'dp')), parts along dimension 0
- grad_scalars: float32 [4], P('group'), parts along dimension 0
There are 2 independent parts, one for each index of `group`. A program takes and returns all parts, laid end to end along the dimension named above; an argument that names none is the same for every part. Nothing has to cross between parts.
Inputs may be any that keep to these rules, and one draw needn't show every extreme that they name: `positives`: two sentence ids for each clip; they may coincide.
All inputs are finite; a program needn't handle non-finite values.
Results may differ from a plain program's by a relative error of at most 0.002.
The roundings to bfloat16 on the way count: a program that leaves them out, or rounds other values in their place, can miss the bound.
Values may be sent and summed in bfloat16 or wider, within the bound.
A program may use at most 64 MiB of HBM per device.

v0:
```python
import jax
import jax.numpy as jnp
from jax import lax
from jax.sharding import PartitionSpec as P

column_block = 2048


def swapped(x, axis, apart):
    return lax.ppermute(x, axis, [(i, i ^ 1 << apart) for i in range(lax.axis_size(axis))])


def shards(clips_feat, weight, sentences, log_scale, bias, positives):
    rows_here = clips_feat.shape[0]
    embed_width = weight.shape[1]
    devices = lax.axis_size("dp")
    position = lax.axis_index("dp")
    full_weight = lax.all_gather(weight, "dp", axis=0, tiled=True)
    proj = jnp.dot(clips_feat, full_weight, preferred_element_type=jnp.float32)
    inverse = lax.rsqrt(jnp.sum(proj * proj, axis=1, keepdims=True) + 1e-06)
    unit32 = proj * inverse
    clip_unit = unit32.astype(jnp.bfloat16)
    sent32 = sentences.astype(jnp.float32)
    sent_unit = (
        sent32 * lax.rsqrt(jnp.sum(sent32 * sent32, axis=1, keepdims=True) + 1e-06)
    ).astype(jnp.bfloat16)
    scale = jnp.exp(log_scale[0])
    shift = bias[0]
    inv_count = 1.0 / (rows_here * devices)
    first_pos = positives[:, 0:1]
    second_pos = positives[:, 1:2]

    def one_tile(carry, block, start):
        losses, grad, dscale, dbias = carry
        span = block.shape[0]
        products = lax.dot_general(
            clip_unit, block, (((1,), (1,)), ((), ())), preferred_element_type=jnp.float32
        )
        logits = scale * products + shift
        columns = start + lax.iota(jnp.int32, span)
        matched = (first_pos == columns[None, :]) | (second_pos == columns[None, :])
        target = jnp.where(matched, jnp.float32(1.0), jnp.float32(-1.0))
        margin = target * logits
        losses = losses - jnp.sum(jax.nn.log_sigmoid(margin), axis=1)
        grad_logit = -target * jax.nn.sigmoid(-margin) * inv_count
        dscale = dscale + jnp.sum(grad_logit * (scale * products))
        dbias = dbias + jnp.sum(grad_logit)
        grad = grad + jnp.dot(
            grad_logit.astype(jnp.bfloat16), block, preferred_element_type=jnp.float32
        )
        return (losses, grad, dscale, dbias)

    def tile_rows(carry, piece, start):
        span = piece.shape[0]
        if span > column_block and span % column_block == 0:
            stacked = piece.reshape(span // column_block, column_block, embed_width)
            offsets = start + column_block * lax.iota(jnp.int32, span // column_block)

            def step_once(inner_carry, inputs):
                return (one_tile(inner_carry, inputs[0], inputs[1]), None)

            result, unused = lax.scan(step_once, carry, (stacked, offsets))
            return result
        return one_tile(carry, piece, start)

    initial = (
        jnp.zeros((rows_here,), jnp.float32),
        jnp.zeros((rows_here, embed_width), jnp.float32),
        jnp.float32(0.0),
        jnp.float32(0.0),
    )
    carry = tile_rows(initial, sent_unit, position * rows_here)
    buffer = sent_unit
    levels = devices.bit_length() - 1
    for level in range(levels):
        other = swapped(buffer, "dp", level)
        stride = 1 << level
        partner_base = jnp.bitwise_xor(position, stride) // stride * stride
        carry = tile_rows(carry, other, partner_base * rows_here)
        if level + 1 < levels:
            upper = position // stride % 2 == 1
            buffer = jnp.where(
                upper,
                jnp.concatenate([other, buffer], axis=0),
                jnp.concatenate([buffer, other], axis=0),
            )
    clip_loss, grad, dscale, dbias = carry
    grad_unit = scale * grad
    inner = jnp.sum(unit32 * grad_unit, axis=1, keepdims=True)
    grad_proj = (inverse * (grad_unit - unit32 * inner)).astype(jnp.bfloat16)
    grad_weight = lax.psum_scatter(
        lax.dot_general(
            clips_feat, grad_proj, (((0,), (0,)), ((), ())), preferred_element_type=jnp.float32
        ),
        "dp",
        scatter_dimension=0,
        tiled=True,
    )
    summed = lax.psum((dscale, dbias), "dp")
    grad_scalars = jnp.stack([summed[0], summed[1]])
    return (clip_loss, grad_weight, grad_scalars)


def solution(mesh):
    in_specs = (
        P(("group", "dp"), None),
        P("dp", None),
        P(("group", "dp"), None),
        P(),
        P(),
        P(("group", "dp"), None),
    )
    out_specs = (P(("group", "dp")), P(("group", "dp"), None), P("group"))
    return jax.shard_map(shards, mesh=mesh, in_specs=in_specs, out_specs=out_specs, check_vma=False)
```

profile of v0, /device:TPU:0, one launch (start us, length us, event | category | flops | bytes accessed | tf_op | source)
XLA Modules:
  0.0 191.8 jit_solution(283245672790788973)
XLA Ops:
  7.2 0.7 all-gather.2.cloned.1.call-update
  8.0 1.0 fusion.12
  9.0 1.0 fusion.13
  10.0 0.5 collective-permute-start
  11.9 2.7 %collective-permute-start.1 = (bf16[256,384]{1,0:T(8,128)(2,1)S(1)}, bf16[256,384]{1,0:T(8,128)(2,1)S(1)}, u32[]{:S(2)}, u32[]{:S(2)}) collective-permute-start(bf16[256,384]{1,0:T(8,128)(2,1)S(1)} %maximum_select_fusion.2), channel_id=1, source_target_pairs={{0,2},{1,3},{2,0},{3,1},{4,6},{5,7},{6,4},{7,5},{8,10},{9,11},{10,... | collective-permute-start | bytes 589832 | tf_op jit(solution)/shard_map/ppermute | solution.py:10
  14.6 5.4 %collective-permute-done.1 = bf16[256,384]{1,0:T(8,128)(2,1)S(1)} collective-permute-done((bf16[256,384]{1,0:T(8,128)(2,1)S(1)}, bf16[256,384]{1,0:T(8,128)(2,1)S(1)}, u32[]{:S(2)}, u32[]{:S(2)}) %collective-permute-start.1) | collective-permute-done | bytes 196640 | tf_op jit(solution)/shard_map/ppermute | solution.py:10
  20.0 0.1 maximum_select_fusion.1
  20.2 1.9 collective-permute-start.2
  22.1 0.8 slice_bitcast_fusion.1
  22.8 14.6 %collective-permute-done.2 = bf16[512,384]{1,0:T(8,128)(2,1)S(1)} collective-permute-done((bf16[512,384]{1,0:T(8,128)(2,1)S(1)}, bf16[512,384]{1,0:T(8,128)(2,1)S(1)}, u32[]{:S(2)}, u32[]{:S(2)}) %collective-permute-start.2) | collective-permute-done | bytes 393248 | tf_op jit(solution)/shard_map/ppermute | solution.py:10
  37.4 0.3 maximum_select_fusion
  37.7 2.7 %collective-permute-start.3 = (bf16[1024,384]{1,0:T(8,128)(2,1)S(1)}, bf16[1024,384]{1,0:T(8,128)(2,1)S(1)}, u32[]{:S(2)}, u32[]{:S(2)}) collective-permute-start(bf16[1024,384]{1,0:T(8,128)(2,1)S(1)} %maximum_select_fusion), channel_id=1, source_target_pairs={{0,8},{1,9},{2,10},{3,11},{4,12},{5,13},{6,14},{7,15},{8,0},{9,1},... | collective-permute-start | bytes 2359304 | tf_op jit(solution)/shard_map/ppermute | solution.py:10
  40.4 39.4 %all-gather.2.cloned.1.call-done = bf16[4096,384]{1,0:T(8,128)(2,1)} async-done(((bf16[256,384]{1,0:T(8,128)(2,1)}), bf16[4096,384]{1,0:T(8,128)(2,1)}) %all-gather.2.cloned.1.call-update) | async-done | bytes 3145744 | tf_op jit(solution)/shard_map/all_gather | solution.py:18
  79.8 2.7 %multiply_reduce_fusion.3 = (f32[128]{0:T(128)S(1)}, f32[128,384]{1,0:T(8,128)S(1)}) fusion(bf16[128,4096]{1,0:T(8,128)(2,1)S(1)} %copy-done, bf16[4096,384]{1,0:T(8,128)(2,1)} %all-gather.2.cloned.1.call-done), kind=kOutput, calls=%fused_computation.39 | convolution fusion | flops 402751360 | bytes 4391424 | tf_op jit(solution)/shard_map/dot_general | solution.py:19
  82.5 0.1 multiply_convert_fusion.1
  82.6 0.2 convolution_multiply_fusion.4
  82.8 0.3 fusion.30
  83.1 3.7 %collective-permute-done.3 = bf16[1024,384]{1,0:T(8,128)(2,1)S(1)} collective-permute-done((bf16[1024,384]{1,0:T(8,128)(2,1)S(1)}, bf16[1024,384]{1,0:T(8,128)(2,1)S(1)}, u32[]{:S(2)}, u32[]{:S(2)}) %collective-permute-start.3) | collective-permute-done | bytes 786464 | tf_op jit(solution)/shard_map/ppermute | solution.py:10
  86.7 1.5 multiply_reduce_fusion
  88.2 0.3 fusion.10
  88.5 1.0 multiply_reduce_fusion.5
  89.5 1.0 multiply_reduce_fusion.4
  90.5 0.3 fusion.27
  90.7 1.2 multiply_reduce_fusion.1
  91.9 0.3 fusion.17
  92.2 0.4 multiply_reduce_fusion.2
  92.6 3.8 %convolution_bitcast_fusion = f32[4096,384]{0,1:T(8,128)} fusion(bf16[128,4096]{1,0:T(8,128)(2,1)S(1)} %copy-done, f32[128,384]{1,0:T(8,128)S(1)} %get-tuple-element.35, f32[128,384]{1,0:T(8,128)S(1)} %get-tuple-element.30, f32[128]{0:T(128)S(1)} %get-tuple-element.34, f32[128]{0:T(128)S(1)} %add_rsqrt_fusion.1), kind=kOutput, calls=%fused_computation | convolution fusion | flops 402898944 | bytes 7734272 | tf_op jit(solution)/shard_map/dot_general | solution.py:92
  102.9 35.8 %all-reduce = (f32[1]{0:T(128)}, f32[1]{0:T(128)}) all-reduce(f32[1]{0:T(128)} %bitcast.6, f32[1]{0:T(128)} %bitcast.5), channel_id=1, replica_groups=mesh['group'=2,'dp'=16] {'dp'}, use_global_device_ids=true, to_apply=%region_20.21 | all-reduce | flops 2 | bytes 16 | tf_op jit(solution)/shard_map/psum | solution.py:99
  138.7 1.9 pad_maximum_fusion
  140.6 0.5 negate_subtract_fusion
  141.1 42.0 %reduce-scatter.2.cloned.1.call-done = f32[256,384]{0,1:T(8,128)} async-done(((f32[4096,384]{0,1:T(8,128)}), f32[256,384]{0,1:T(8,128)}) %reduce-scatter.2.cloned.1.call-update) | async-done | bytes 393232 | tf_op jit(solution)/shard_map/reduce_scatter | solution.py:91
  183.1 1.9 copy.9
  (13 shorter events, 0.2 us)
Async XLA Ops:
  7.2 72.6 %copy-start = (bf16[128,4096]{1,0:T(8,128)(2,1)S(1)}, bf16[128,4096]{1,0:T(8,128)(2,1)}, u32[]{:S(2)}) copy-start(bf16[128,4096]{1,0:T(8,128)(2,1)} %param.6) | copy-start | bytes 3145732
  7.2 72.6 %all-gather.2.cloned.1.call-start = ((), (), s32[]{:S(2)}) async-start(), calls=%async_computation.1 | async-start | bytes 3342336 | tf_op jit(solution)/shard_map/all_gather | solution.py:18
  7.9 175.2 %reduce-scatter.2.cloned.1.call-start = ((), (), s32[]{:S(2)}) async-start(), calls=%async_computation.2 | async-start | bytes 6684672 | tf_op jit(solution)/shard_map/reduce_scatter | solution.py:91
  10.0 1.9 collective-permute-start
  11.9 8.1 %collective-permute-start.1 = (bf16[256,384]{1,0:T(8,128)(2,1)S(1)}, bf16[256,384]{1,0:T(8,128)(2,1)S(1)}, u32[]{:S(2)}, u32[]{:S(2)}) collective-permute-start(bf16[256,384]{1,0:T(8,128)(2,1)S(1)} %maximum_select_fusion.2), channel_id=1, source_target_pairs={{0,2},{1,3},{2,0},{3,1},{4,6},{5,7},{6,4},{7,5},{8,10},{9,11},{10,... | collective-permute-start | bytes 589832 | tf_op jit(solution)/shard_map/ppermute | solution.py:10
  20.2 17.2 %collective-permute-start.2 = (bf16[512,384]{1,0:T(8,128)(2,1)S(1)}, bf16[512,384]{1,0:T(8,128)(2,1)S(1)}, u32[]{:S(2)}, u32[]{:S(2)}) collective-permute-start(bf16[512,384]{1,0:T(8,128)(2,1)S(1)} %maximum_select_fusion.1), channel_id=1, source_target_pairs={{0,4},{1,5},{2,6},{3,7},{4,0},{5,1},{6,2},{7,3},{8,12},{9,13},{10,... | collective-permute-start | bytes 1179656 | tf_op jit(solution)/shard_map/ppermute | solution.py:10
  37.7 49.0 %collective-permute-start.3 = (bf16[1024,384]{1,0:T(8,128)(2,1)S(1)}, bf16[1024,384]{1,0:T(8,128)(2,1)S(1)}, u32[]{:S(2)}, u32[]{:S(2)}) collective-permute-start(bf16[1024,384]{1,0:T(8,128)(2,1)S(1)} %maximum_select_fusion), channel_id=1, source_target_pairs={{0,8},{1,9},{2,10},{3,11},{4,12},{5,13},{6,14},{7,15},{8,0},{9,1},... | collective-permute-start | bytes 2359304 | tf_op jit(solution)/shard_map/ppermute | solution.py:10
Sparse Core Ops, SparseCore 0:
  10.3 69.4 all-gather.1
  96.6 86.4 reduce-scatter.1
where the time goes:
time: 192 us
  waiting for transfers between devices  106 us (55%)
  blocking collectives  35.8 us (19%)
  between operations  22 us (11%)
  matrix products  12.8 us (7%)
  starting transfers between devices  7.85 us (4%)
  other arithmetic  4.99 us (3%)
  local copies, waits for them, and re-layouts  2.67 us (1%)
    reduce_scatter x1, waiting for transfers between devices, shards(): lax.psum_scatter(lax.dot_general(clips_feat, grad_proj, (((0,), (0,)), ((...  42 us
    all_gather x1, waiting for transfers between devices, shards(): full_weight = lax.all_gather(weight, 'dp', axis=0, tiled=True)  39.4 us
    psum x1, blocking collectives, shards(): summed = lax.psum((dscale, dbias), 'dp')  35.8 us
    ppermute x4, waiting for transfers between devices, swapped(): lax.ppermute(x, axis, [(i, i ^ 1 << apart) for i in range(lax.axis_size(a...  23.6 us
    ppermute x4, starting transfers between devices, swapped(): lax.ppermute(x, axis, [(i, i ^ 1 << apart) for i in range(lax.axis_size(a...  7.77 us
    dot_general x5, matrix products, one_tile(): lax.dot_general(clip_unit, block, (((1,), (1,)), ((), ())), preferred_ele...  4.8 us
  transfers between devices with their start and end apart: 6, of which 5 were waited for; matrix products, arithmetic and copies ran while one was open for 5% of the time, Pallas kernels for 0%

commit v1 on v0

--- a/solution.py
+++ b/solution.py
@@ -15,7 +15,12 @@
     embed_width = weight.shape[1]
     devices = lax.axis_size("dp")
     position = lax.axis_index("dp")
-    full_weight = lax.all_gather(weight, "dp", axis=0, tiled=True)
+    ring = [weight]
+    for hop in range(15):
+        ring.append(lax.ppermute(ring[-1], "dp", [(dev, (dev + 1) % 16) for dev in range(16)]))
+    full_weight = jnp.roll(
+        jnp.concatenate(ring[::-1], axis=0), (lax.axis_index("dp") + 1) * ring[0].shape[0], axis=0
+    )
     proj = jnp.dot(clips_feat, full_weight, preferred_element_type=jnp.float32)
     inverse = lax.rsqrt(jnp.sum(proj * proj, axis=1, keepdims=True) + 1e-06)
     unit32 = proj * inverse

time: 192 us -> 257 us (1.34)
  waiting for transfers between devices: 106 us -> 172 us
  starting transfers between devices: 7.85 us -> 0.86 us
  blocking collectives: 35.8 us -> 38.7 us
    ppermute x0 -> x15, waiting for transfers between devices: none -> 114 us  [shards(): lax.ppermute(ring[-1], 'dp', [(dev, (dev + 1) % 16) for dev in range(16)])]
    all_gather x1 -> x0, waiting for transfers between devices: 39.4 us -> none  [shards(): full_weight = lax.all_gather(weight, 'dp', axis=0, tiled=True)]
    ppermute x4, waiting for transfers between devices: 23.6 us -> 15.6 us  [swapped(): lax.ppermute(x, axis, [(i, i ^ 1 << apart) for i in range(lax.axis_size(a...]
    ppermute x4, starting transfers between devices: 7.77 us -> 0.29 us  [swapped(): lax.ppermute(x, axis, [(i, i ^ 1 << apart) for i in range(lax.axis_size(a...]
    psum x1, blocking collectives: 35.8 us -> 38.7 us  [shards(): summed = lax.psum((dscale, dbias), 'dp')]
  transfers between devices with their start and end apart: 6 -> 20, of which waited for: 5 -> 17; matrix products, arithmetic and copies ran while one was open for 5% -> 4% of each run, Pallas kernels for 0% -> 0%
where the time goes in v1:
time: 257 us
  waiting for transfers between devices  172 us (67%)
  blocking collectives  38.7 us (15%)
  between operations  22.3 us (9%)
  matrix products  13 us (5%)
  other arithmetic  5.89 us (2%)
  local copies, waits for them, and re-layouts  3.73 us (1%)
    ppermute x15, waiting for transfers between devices, shards(): lax.ppermute(ring[-1], 'dp', [(dev, (dev + 1) % 16) for dev in range(16)])  114 us
    reduce_scatter x1, waiting for transfers between devices, shards(): lax.psum_scatter(lax.dot_general(clips_feat, grad_proj, (((0,), (0,)), ((...  42.4 us
    psum x1, blocking collectives, shards(): summed = lax.psum((dscale, dbias), 'dp')  38.7 us
    ppermute x4, waiting for transfers between devices, swapped(): lax.ppermute(x, axis, [(i, i ^ 1 << apart) for i in range(lax.axis_size(a...  15.6 us
    dot_general x5, matrix products, one_tile(): lax.dot_general(clip_unit, block, (((1,), (1,)), ((), ())), preferred_ele...  5.67 us
  transfers between devices with their start and end apart: 20, of which 17 were waited for; matrix products, arithmetic and copies ran while one was open for 4% of the time, Pallas kernels for 0%

profile of v1, /device:TPU:0, one launch (start us, length us, event | category | flops | bytes accessed | tf_op | source)
XLA Modules:
  0.0 256.7 jit_solution(2316912348758481467)
XLA Ops:
  7.7 8.5 %collective-permute-done = bf16[256,384]{1,0:T(8,128)(2,1)S(1)} collective-permute-done((bf16[256,384]{1,0:T(8,128)(2,1)}, bf16[256,384]{1,0:T(8,128)(2,1)S(1)}, u32[]{:S(2)}, u32[]{:S(2)}) %collective-permute-start) | collective-permute-done | bytes 196640 | tf_op jit(solution)/shard_map/ppermute | solution.py:20
  16.3 7.8 %collective-permute-done.1 = bf16[256,384]{1,0:T(8,128)(2,1)S(1)} collective-permute-done((bf16[256,384]{1,0:T(8,128)(2,1)S(1)}, bf16[256,384]{1,0:T(8,128)(2,1)S(1)}, u32[]{:S(2)}, u32[]{:S(2)}) %collective-permute-start.1) | collective-permute-done | bytes 196640 | tf_op jit(solution)/shard_map/ppermute | solution.py:20
  24.1 7.8 %collective-permute-done.2 = bf16[256,384]{1,0:T(8,128)(2,1)S(1)} collective-permute-done((bf16[256,384]{1,0:T(8,128)(2,1)S(1)}, bf16[256,384]{1,0:T(8,128)(2,1)S(1)}, u32[]{:S(2)}, u32[]{:S(2)}) %collective-permute-start.2) | collective-permute-done | bytes 196640 | tf_op jit(solution)/shard_map/ppermute | solution.py:20
  31.9 7.8 %collective-permute-done.3 = bf16[256,384]{1,0:T(8,128)(2,1)S(1)} collective-permute-done((bf16[256,384]{1,0:T(8,128)(2,1)S(1)}, bf16[256,384]{1,0:T(8,128)(2,1)S(1)}, u32[]{:S(2)}, u32[]{:S(2)}) %collective-permute-start.3) | collective-permute-done | bytes 196640 | tf_op jit(solution)/shard_map/ppermute | solution.py:20
  39.6 7.8 %collective-permute-done.4 = bf16[256,384]{1,0:T(8,128)(2,1)S(1)} collective-permute-done((bf16[256,384]{1,0:T(8,128)(2,1)S(1)}, bf16[256,384]{1,0:T(8,128)(2,1)S(1)}, u32[]{:S(2)}, u32[]{:S(2)}) %collective-permute-start.4) | collective-permute-done | bytes 196640 | tf_op jit(solution)/shard_map/ppermute | solution.py:20
  47.4 7.8 %collective-permute-done.5 = bf16[256,384]{1,0:T(8,128)(2,1)S(1)} collective-permute-done((bf16[256,384]{1,0:T(8,128)(2,1)S(1)}, bf16[256,384]{1,0:T(8,128)(2,1)S(1)}, u32[]{:S(2)}, u32[]{:S(2)}) %collective-permute-start.5) | collective-permute-done | bytes 196640 | tf_op jit(solution)/shard_map/ppermute | solution.py:20
  55.2 7.8 %collective-permute-done.6 = bf16[256,384]{1,0:T(8,128)(2,1)S(1)} collective-permute-done((bf16[256,384]{1,0:T(8,128)(2,1)S(1)}, bf16[256,384]{1,0:T(8,128)(2,1)S(1)}, u32[]{:S(2)}, u32[]{:S(2)}) %collective-permute-start.6) | collective-permute-done | bytes 196640 | tf_op jit(solution)/shard_map/ppermute | solution.py:20
  63.0 1.0 fusion.14
  64.0 6.8 %collective-permute-done.7 = bf16[256,384]{1,0:T(8,128)(2,1)S(1)} collective-permute-done((bf16[256,384]{1,0:T(8,128)(2,1)S(1)}, bf16[256,384]{1,0:T(8,128)(2,1)S(1)}, u32[]{:S(2)}, u32[]{:S(2)}) %collective-permute-start.7) | collective-permute-done | bytes 196640 | tf_op jit(solution)/shard_map/ppermute | solution.py:20
  70.8 7.8 %collective-permute-done.8 = bf16[256,384]{1,0:T(8,128)(2,1)S(1)} collective-permute-done((bf16[256,384]{1,0:T(8,128)(2,1)S(1)}, bf16[256,384]{1,0:T(8,128)(2,1)S(1)}, u32[]{:S(2)}, u32[]{:S(2)}) %collective-permute-start.8) | collective-permute-done | bytes 196640 | tf_op jit(solution)/shard_map/ppermute | solution.py:20
  78.6 1.0 fusion.15
  79.7 6.8 %collective-permute-done.9 = bf16[256,384]{1,0:T(8,128)(2,1)S(1)} collective-permute-done((bf16[256,384]{1,0:T(8,128)(2,1)S(1)}, bf16[256,384]{1,0:T(8,128)(2,1)S(1)}, u32[]{:S(2)}, u32[]{:S(2)}) %collective-permute-start.9) | collective-permute-done | bytes 196640 | tf_op jit(solution)/shard_map/ppermute | solution.py:20
  87.9 1.0 maximum_select_fusion.2
  89.0 5.4 %collective-permute-done.10 = bf16[256,384]{1,0:T(8,128)(2,1)S(1)} collective-permute-done((bf16[256,384]{1,0:T(8,128)(2,1)S(1)}, bf16[256,384]{1,0:T(8,128)(2,1)S(1)}, u32[]{:S(2)}, u32[]{:S(2)}) %collective-permute-start.10) | collective-permute-done | bytes 196640 | tf_op jit(solution)/shard_map/ppermute | solution.py:20
  94.4 7.9 %collective-permute-done.11 = bf16[256,384]{1,0:T(8,128)(2,1)S(1)} collective-permute-done((bf16[256,384]{1,0:T(8,128)(2,1)S(1)}, bf16[256,384]{1,0:T(8,128)(2,1)S(1)}, u32[]{:S(2)}, u32[]{:S(2)}) %collective-permute-start.11) | collective-permute-done | bytes 196640 | tf_op jit(solution)/shard_map/ppermute | solution.py:20
  102.5 7.5 %collective-permute-done.12 = bf16[256,384]{1,0:T(8,128)(2,1)S(1)} collective-permute-done((bf16[256,384]{1,0:T(8,128)(2,1)S(1)}, bf16[256,384]{1,0:T(8,128)(2,1)S(1)}, u32[]{:S(2)}, u32[]{:S(2)}) %collective-permute-start.12) | collective-permute-done | bytes 196640 | tf_op jit(solution)/shard_map/ppermute | solution.py:20
  110.1 0.8 slice_bitcast_fusion.1
  110.9 7.1 %collective-permute-done.13 = bf16[256,384]{1,0:T(8,128)(2,1)S(1)} collective-permute-done((bf16[256,384]{1,0:T(8,128)(2,1)S(1)}, bf16[256,384]{1,0:T(8,128)(2,1)S(1)}, u32[]{:S(2)}, u32[]{:S(2)}) %collective-permute-start.13) | collective-permute-done | bytes 196640 | tf_op jit(solution)/shard_map/ppermute | solution.py:20
  118.4 9.6 %collective-permute-done.14 = bf16[256,384]{1,0:T(8,128)(2,1)S(1)} collective-permute-done((bf16[256,384]{1,0:T(8,128)(2,1)S(1)}, bf16[256,384]{1,0:T(8,128)(2,1)S(1)}, u32[]{:S(2)}, u32[]{:S(2)}) %collective-permute-start.14) | collective-permute-done | bytes 196640 | tf_op jit(solution)/shard_map/ppermute | solution.py:20
  129.3 1.1 multiply_reduce_fusion.2
  130.9 15.6 %collective-permute-done.18 = bf16[1024,384]{1,0:T(8,128)(2,1)S(1)} collective-permute-done((bf16[1024,384]{1,0:T(8,128)(2,1)S(1)}, bf16[1024,384]{1,0:T(8,128)(2,1)S(1)}, u32[]{:S(2)}, u32[]{:S(2)}) %collective-permute-start.18) | collective-permute-done | bytes 786464 | tf_op jit(solution)/shard_map/ppermute | solution.py:10
  146.5 1.5 multiply_reduce_fusion
  148.4 1.8 multiply_reduce_fusion.4
  150.2 1.0 multiply_reduce_fusion.3
  151.2 1.2 multiply_reduce_fusion.1
  153.2 1.2 fusion.16
  154.4 3.6 %convolution_bitcast_fusion = f32[4096,384]{0,1:T(8,128)} fusion(bf16[128,4096]{1,0:T(8,128)(2,1)S(1)} %copy-done, f32[128,384]{0,1:T(8,128)S(1)} %get-tuple-element.35, f32[384,128]{1,0:T(8,128)S(1)} %get-tuple-element.30, f32[128]{0:T(128)S(1)} %get-tuple-element.34, f32[128]{0:T(128)S(1)} %add_rsqrt_fusion.1), kind=kOutput, calls=%fused_computation | convolution fusion | flops 402898944 | bytes 7734272 | tf_op jit(solution)/shard_map/dot_general | solution.py:97
  164.5 38.7 %all-reduce = (f32[1]{0:T(128)}, f32[1]{0:T(128)}) all-reduce(f32[1]{0:T(128)} %bitcast.7, f32[1]{0:T(128)} %bitcast.6), channel_id=1, replica_groups=mesh['group'=2,'dp'=16] {'dp'}, use_global_device_ids=true, to_apply=%region_20.21 | all-reduce | flops 2 | bytes 16 | tf_op jit(solution)/shard_map/psum | solution.py:104
  203.2 1.9 pad_maximum_fusion
  205.0 0.5 negate_subtract_fusion
  205.6 42.4 %reduce-scatter.2.cloned.1.call-done = f32[256,384]{0,1:T(8,128)} async-done(((f32[4096,384]{0,1:T(8,128)}), f32[256,384]{0,1:T(8,128)}) %reduce-scatter.2.cloned.1.call-update) | async-done | bytes 393232 | tf_op jit(solution)/shard_map/reduce_scatter | solution.py:96
  248.0 1.9 copy.14
  (74 shorter events, 4.1 us)
Async XLA Ops:
  7.2 122.1 %copy-start = (bf16[128,4096]{1,0:T(8,128)(2,1)S(1)}, bf16[128,4096]{1,0:T(8,128)(2,1)}, u32[]{:S(2)}) copy-start(bf16[128,4096]{1,0:T(8,128)(2,1)} %param.6) | copy-start | bytes 3145732
  7.2 121.4 %copy-start.1 = (bf16[256,384]{1,0:T(8,128)(2,1)S(1)}, bf16[256,384]{1,0:T(8,128)(2,1)}, u32[]{:S(2)}) copy-start(bf16[256,384]{1,0:T(8,128)(2,1)} %param.7) | copy-start | bytes 589828
  7.2 240.8 %reduce-scatter.2.cloned.1.call-start = ((), (), s32[]{:S(2)}) async-start(), calls=%async_computation.1 | async-start | bytes 6684672 | tf_op jit(solution)/shard_map/reduce_scatter | solution.py:96
  7.2 9.0 %collective-permute-start = (bf16[256,384]{1,0:T(8,128)(2,1)}, bf16[256,384]{1,0:T(8,128)(2,1)S(1)}, u32[]{:S(2)}, u32[]{:S(2)}) collective-permute-start(bf16[256,384]{1,0:T(8,128)(2,1)} %param.7), channel_id=1, source_target_pairs={{0,1},{1,2},{2,3},{3,4},{4,5},{5,6},{6,7},{7,8},{8,9},{9,10},{10,1... | collective-permute-start | bytes 589832 | tf_op jit(solution)/shard_map/ppermute | solution.py:20
  16.3 7.8 %collective-permute-start.1 = (bf16[256,384]{1,0:T(8,128)(2,1)S(1)}, bf16[256,384]{1,0:T(8,128)(2,1)S(1)}, u32[]{:S(2)}, u32[]{:S(2)}) collective-permute-start(bf16[256,384]{1,0:T(8,128)(2,1)S(1)} %collective-permute-done), channel_id=1, source_target_pairs={{0,1},{1,2},{2,3},{3,4},{4,5},{5,6},{6,7},{7,8},{8,9},{9,10},{10,1... | collective-permute-start | bytes 589832 | tf_op jit(solution)/shard_map/ppermute | solution.py:20
  24.1 7.8 %collective-permute-start.2 = (bf16[256,384]{1,0:T(8,128)(2,1)S(1)}, bf16[256,384]{1,0:T(8,128)(2,1)S(1)}, u32[]{:S(2)}, u32[]{:S(2)}) collective-permute-start(bf16[256,384]{1,0:T(8,128)(2,1)S(1)} %collective-permute-done.1), channel_id=1, source_target_pairs={{0,1},{1,2},{2,3},{3,4},{4,5},{5,6},{6,7},{7,8},{8,9},{9,10},{10,1... | collective-permute-start | bytes 589832 | tf_op jit(solution)/shard_map/ppermute | solution.py:20
  31.9 7.8 %collective-permute-start.3 = (bf16[256,384]{1,0:T(8,128)(2,1)S(1)}, bf16[256,384]{1,0:T(8,128)(2,1)S(1)}, u32[]{:S(2)}, u32[]{:S(2)}) collective-permute-start(bf16[256,384]{1,0:T(8,128)(2,1)S(1)} %collective-permute-done.2), channel_id=1, source_target_pairs={{0,1},{1,2},{2,3},{3,4},{4,5},{5,6},{6,7},{7,8},{8,9},{9,10},{10,1... | collective-permute-start | bytes 589832 | tf_op jit(solution)/shard_map/ppermute | solution.py:20
  39.6 7.8 %collective-permute-start.4 = (bf16[256,384]{1,0:T(8,128)(2,1)S(1)}, bf16[256,384]{1,0:T(8,128)(2,1)S(1)}, u32[]{:S(2)}, u32[]{:S(2)}) collective-permute-start(bf16[256,384]{1,0:T(8,128)(2,1)S(1)} %collective-permute-done.3), channel_id=1, source_target_pairs={{0,1},{1,2},{2,3},{3,4},{4,5},{5,6},{6,7},{7,8},{8,9},{9,10},{10,1... | collective-permute-start | bytes 589832 | tf_op jit(solution)/shard_map/ppermute | solution.py:20
  47.4 7.8 %collective-permute-start.5 = (bf16[256,384]{1,0:T(8,128)(2,1)S(1)}, bf16[256,384]{1,0:T(8,128)(2,1)S(1)}, u32[]{:S(2)}, u32[]{:S(2)}) collective-permute-start(bf16[256,384]{1,0:T(8,128)(2,1)S(1)} %collective-permute-done.4), channel_id=1, source_target_pairs={{0,1},{1,2},{2,3},{3,4},{4,5},{5,6},{6,7},{7,8},{8,9},{9,10},{10,1... | collective-permute-start | bytes 589832 | tf_op jit(solution)/shard_map/ppermute | solution.py:20
  55.2 7.8 %collective-permute-start.6 = (bf16[256,384]{1,0:T(8,128)(2,1)S(1)}, bf16[256,384]{1,0:T(8,128)(2,1)S(1)}, u32[]{:S(2)}, u32[]{:S(2)}) collective-permute-start(bf16[256,384]{1,0:T(8,128)(2,1)S(1)} %collective-permute-done.5), channel_id=1, source_target_pairs={{0,1},{1,2},{2,3},{3,4},{4,5},{5,6},{6,7},{7,8},{8,9},{9,10},{10,1... | collective-permute-start | bytes 589832 | tf_op jit(solution)/shard_map/ppermute | solution.py:20
  63.0 7.8 %collective-permute-start.7 = (bf16[256,384]{1,0:T(8,128)(2,1)S(1)}, bf16[256,384]{1,0:T(8,128)(2,1)S(1)}, u32[]{:S(2)}, u32[]{:S(2)}) collective-permute-start(bf16[256,384]{1,0:T(8,128)(2,1)S(1)} %collective-permute-done.6), channel_id=1, source_target_pairs={{0,1},{1,2},{2,3},{3,4},{4,5},{5,6},{6,7},{7,8},{8,9},{9,10},{10,1... | collective-permute-start | bytes 589832 | tf_op jit(solution)/shard_map/ppermute | solution.py:20
  70.8 7.8 %collective-permute-start.8 = (bf16[256,384]{1,0:T(8,128)(2,1)S(1)}, bf16[256,384]{1,0:T(8,128)(2,1)S(1)}, u32[]{:S(2)}, u32[]{:S(2)}) collective-permute-start(bf16[256,384]{1,0:T(8,128)(2,1)S(1)} %collective-permute-done.7), channel_id=1, source_target_pairs={{0,1},{1,2},{2,3},{3,4},{4,5},{5,6},{6,7},{7,8},{8,9},{9,10},{10,1... | collective-permute-start | bytes 589832 | tf_op jit(solution)/shard_map/ppermute | solution.py:20
  78.6 7.9 %collective-permute-start.9 = (bf16[256,384]{1,0:T(8,128)(2,1)S(1)}, bf16[256,384]{1,0:T(8,128)(2,1)S(1)}, u32[]{:S(2)}, u32[]{:S(2)}) collective-permute-start(bf16[256,384]{1,0:T(8,128)(2,1)S(1)} %collective-permute-done.8), channel_id=1, source_target_pairs={{0,1},{1,2},{2,3},{3,4},{4,5},{5,6},{6,7},{7,8},{8,9},{9,10},{10,1... | collective-permute-start | bytes 589832 | tf_op jit(solution)/shard_map/ppermute | solution.py:20
  79.6 8.3 %collective-permute-start.15 = (bf16[128,384]{1,0:T(8,128)(2,1)S(1)}, bf16[128,384]{1,0:T(8,128)(2,1)}, u32[]{:S(2)}, u32[]{:S(2)}) collective-permute-start(bf16[128,384]{1,0:T(8,128)(2,1)S(1)} %fusion.15), channel_id=1, source_target_pairs={{0,1},{1,0},{2,3},{3,2},{4,5},{5,4},{6,7},{7,6},{8,9},{9,8},{10,11... | collective-permute-start | bytes 294920 | tf_op jit(solution)/shard_map/ppermute | solution.py:10
  86.5 7.9 %collective-permute-start.10 = (bf16[256,384]{1,0:T(8,128)(2,1)S(1)}, bf16[256,384]{1,0:T(8,128)(2,1)S(1)}, u32[]{:S(2)}, u32[]{:S(2)}) collective-permute-start(bf16[256,384]{1,0:T(8,128)(2,1)S(1)} %collective-permute-done.9), channel_id=1, source_target_pairs={{0,1},{1,2},{2,3},{3,4},{4,5},{5,6},{6,7},{7,8},{8,9},{9,10},{10,1... | collective-permute-start | bytes 589832 | tf_op jit(solution)/shard_map/ppermute | solution.py:20
  89.0 13.4 %collective-permute-start.16 = (bf16[256,384]{1,0:T(8,128)(2,1)S(1)}, bf16[256,384]{1,0:T(8,128)(2,1)S(1)}, u32[]{:S(2)}, u32[]{:S(2)}) collective-permute-start(bf16[256,384]{1,0:T(8,128)(2,1)S(1)} %maximum_select_fusion.2), channel_id=1, source_target_pairs={{0,2},{1,3},{2,0},{3,1},{4,6},{5,7},{6,4},{7,5},{8,10},{9,11},{10,... | collective-permute-start | bytes 589832 | tf_op jit(solution)/shard_map/ppermute | solution.py:10
  94.4 7.9 %collective-permute-start.11 = (bf16[256,384]{1,0:T(8,128)(2,1)S(1)}, bf16[256,384]{1,0:T(8,128)(2,1)S(1)}, u32[]{:S(2)}, u32[]{:S(2)}) collective-permute-start(bf16[256,384]{1,0:T(8,128)(2,1)S(1)} %collective-permute-done.10), channel_id=1, source_target_pairs={{0,1},{1,2},{2,3},{3,4},{4,5},{5,6},{6,7},{7,8},{8,9},{9,10},{10,1... | collective-permute-start | bytes 589832 | tf_op jit(solution)/shard_map/ppermute | solution.py:20
  102.3 7.8 %collective-permute-start.12 = (bf16[256,384]{1,0:T(8,128)(2,1)S(1)}, bf16[256,384]{1,0:T(8,128)(2,1)S(1)}, u32[]{:S(2)}, u32[]{:S(2)}) collective-permute-start(bf16[256,384]{1,0:T(8,128)(2,1)S(1)} %collective-permute-done.11), channel_id=1, source_target_pairs={{0,1},{1,2},{2,3},{3,4},{4,5},{5,6},{6,7},{7,8},{8,9},{9,10},{10,1... | collective-permute-start | bytes 589832 | tf_op jit(solution)/shard_map/ppermute | solution.py:20
  102.5 15.5 %collective-permute-start.17 = (bf16[512,384]{1,0:T(8,128)(2,1)S(1)}, bf16[512,384]{1,0:T(8,128)(2,1)S(1)}, u32[]{:S(2)}, u32[]{:S(2)}) collective-permute-start(bf16[512,384]{1,0:T(8,128)(2,1)S(1)} %maximum_select_fusion.1), channel_id=1, source_target_pairs={{0,4},{1,5},{2,6},{3,7},{4,0},{5,1},{6,2},{7,3},{8,12},{9,13},{10,... | collective-permute-start | bytes 1179656 | tf_op jit(solution)/shard_map/ppermute | solution.py:10
  110.1 7.9 %collective-permute-start.13 = (bf16[256,384]{1,0:T(8,128)(2,1)S(1)}, bf16[256,384]{1,0:T(8,128)(2,1)S(1)}, u32[]{:S(2)}, u32[]{:S(2)}) collective-permute-start(bf16[256,384]{1,0:T(8,128)(2,1)S(1)} %collective-permute-done.12), channel_id=1, source_target_pairs={{0,1},{1,2},{2,3},{3,4},{4,5},{5,6},{6,7},{7,8},{8,9},{9,10},{10,1... | collective-permute-start | bytes 589832 | tf_op jit(solution)/shard_map/ppermute | solution.py:20
  118.0 10.0 %collective-permute-start.14 = (bf16[256,384]{1,0:T(8,128)(2,1)S(1)}, bf16[256,384]{1,0:T(8,128)(2,1)S(1)}, u32[]{:S(2)}, u32[]{:S(2)}) collective-permute-start(bf16[256,384]{1,0:T(8,128)(2,1)S(1)} %collective-permute-done.13), channel_id=1, source_target_pairs={{0,1},{1,2},{2,3},{3,4},{4,5},{5,6},{6,7},{7,8},{8,9},{9,10},{10,1... | collective-permute-start | bytes 589832 | tf_op jit(solution)/shard_map/ppermute | solution.py:20
  118.3 28.2 %collective-permute-start.18 = (bf16[1024,384]{1,0:T(8,128)(2,1)S(1)}, bf16[1024,384]{1,0:T(8,128)(2,1)S(1)}, u32[]{:S(2)}, u32[]{:S(2)}) collective-permute-start(bf16[1024,384]{1,0:T(8,128)(2,1)S(1)} %maximum_select_fusion), channel_id=1, source_target_pairs={{0,8},{1,9},{2,10},{3,11},{4,12},{5,13},{6,14},{7,15},{8,0},{9,1},... | collective-permute-start | bytes 2359304 | tf_op jit(solution)/shard_map/ppermute | solution.py:10
Sparse Core Ops, SparseCore 0:
  158.2 89.7 reduce-scatter.1
